TPU v7x, 32 devices: a whole 2x2x4 slice. The times are simulated.
32 devices in a mesh: outer: 2 (over x), inner: 16 (over z, y, core).
Axes of the slice: x: 2, y: 2, z: 4, core: 2. Of those that a mesh axis runs over, the one named last changes fastest.
Arguments:
- queries: bfloat16 [4096, 2048], P('inner'), may hold values from -128 to 128
- mem_keys: bfloat16 [512, 2048], P(('outer', 'inner')), may hold values from -4.5 to 4.5
- mem_values: bfloat16 [512, 2048], P(('outer', 'inner')), may hold values from -6 to 6
Outputs:
- attended: bfloat16 [4096, 2048], P('inner')
- log_total: float32 [4096, 16], P('inner')
All inputs are finite; a program needn't handle non-finite values.
Results may differ from a plain program's by a relative error of at most 0.014.
Values may be sent and summed in bfloat16 or wider, within the bound.
A program may use at most 64 MiB of HBM per device.

v0:
```python
import math

import jax
import jax.numpy as jnp
from jax import lax
from jax.sharding import PartitionSpec as P

HEADS = 16
HEAD_DIM = 128


def on_device(queries, mem_keys, mem_values):
    row_count = queries.shape[0]
    columns = queries.shape[1]
    scale = 1.0 / math.sqrt(HEAD_DIM)
    query_heads = queries.reshape(row_count, HEADS, HEAD_DIM)
    initial = (
        jnp.full((row_count, HEADS), -jnp.inf, jnp.float32),
        jnp.zeros((row_count, HEADS), jnp.float32),
        jnp.zeros((row_count, HEADS, HEAD_DIM), jnp.float32),
    )
    key_piece = lax.all_gather(mem_keys, "inner", axis=0, tiled=True)
    value_piece = lax.all_gather(mem_values, "inner", axis=0, tiled=True)
    entries = key_piece.shape[0]
    block = math.gcd(entries, 256)
    key_blocks = key_piece.reshape(entries // block, block, HEADS, HEAD_DIM)
    value_blocks = value_piece.reshape(entries // block, block, HEADS, HEAD_DIM)

    def one_block(running, blocks):
        running_top, running_total, running_out = running
        key_block, value_block = blocks
        scores = (
            jnp.einsum("thd,khd->thk", query_heads, key_block, preferred_element_type=jnp.float32)
            * scale
        )
        new_top = jnp.maximum(running_top, jnp.max(scores, axis=-1))
        fading = jnp.exp(running_top - new_top)
        raw = jnp.exp(scores - new_top[..., None])
        new_total = running_total * fading + jnp.sum(raw, axis=-1)
        product = jnp.einsum(
            "thk,khd->thd",
            raw.astype(jnp.bfloat16),
            value_block,
            preferred_element_type=jnp.float32,
        )
        new_out = running_out * fading[..., None] + product
        return ((new_top, new_total, new_out), None)

    result, unused = lax.scan(one_block, initial, (key_blocks, value_blocks))
    group_peak, group_total, group_out = result
    peak = lax.pmax(group_peak, "outer")
    factor = jnp.exp(group_peak - peak)
    weighted = (group_out * factor[..., None]).reshape(row_count, columns)
    total = lax.psum(group_total * factor, "outer")
    log_total = peak + jnp.log(total)
    summed = lax.psum(weighted.astype(jnp.bfloat16), "outer").astype(jnp.float32)
    attended = (
        (summed.reshape(row_count, HEADS, HEAD_DIM) / total[..., None])
        .astype(jnp.bfloat16)
        .reshape(row_count, columns)
    )
    return (attended, log_total)


def solution(mesh):
    in_specs = (P("inner", None), P(("outer", "inner"), None), P(("outer", "inner"), None))
    out_specs = (P("inner", None), P("inner", None))
    return jax.shard_map(
        on_device, mesh=mesh, in_specs=in_specs, out_specs=out_specs, check_vma=False
    )
```

profile of v0, /device:TPU:0, one launch (start us, length us, event | category | flops | bytes accessed | tf_op | source)
XLA Modules:
  0.0 145.4 jit_solution(7062286540608754651)
XLA Ops:
  7.2 0.0 copy-start
  7.2 0.0 all-gather.3.cloned.1.call-start
  7.2 0.7 all-gather.3.cloned.1.call-update
  7.9 0.0 all-gather.5.cloned.1.call-start
  8.0 0.7 all-gather.5.cloned.1.call-update
  8.7 0.0 all-reduce.2.cloned.1.call-start
  8.7 42.1 %all-gather.3.cloned.1.call-done = bf16[256,2048]{1,0:T(8,128)(2,1)} async-done(((bf16[16,2048]{1,0:T(8,128)(2,1)}), bf16[256,2048]{1,0:T(8,128)(2,1)}) %all-gather.3.cloned.1.call-update) | async-done | bytes 1048592 | tf_op jit(solution)/shard_map/all_gather | solution.py:22
  50.9 1.5 %copy.17 = bf16[256,2048]{0,1:T(8,128)(2,1)S(1)} copy(bf16[256,2048]{1,0:T(8,128)(2,1)} %all-gather.3.cloned.1.call-done) | data formatting | bytes 2097152 | tf_op jit(solution)/shard_map/all_gather | solution.py:22
  52.3 0.0 copy-done
  52.3 2.7 %bitcast_reduce_fusion = (f32[256,16]{0,1:T(8,128)S(1)}, f32[16,256,256]{2,1,0:T(8,128)}) fusion(bf16[256,16,128]{0,2,1:T(8,128)(2,1)S(1)} %bitcast.40, bf16[256,2048]{1,0:T(8,128)(2,1)S(1)} %copy-done), kind=kOutput, calls=%fused_computation.1 | convolution fusion | flops 270528512 | bytes 6307840 | tf_op jit(solution)/shard_map/while/body/eval_jaxpr/thd,khd->thk/dot_general | solution.py:33
  55.1 8.1 %pmax.7 = f32[256,16]{0,1:T(8,128)S(1)} all-reduce(f32[256,16]{0,1:T(8,128)S(1)} %get-tuple-element.19), channel_id=1, replica_groups=mesh['outer'=2,'inner'=16] {'outer'}, use_global_device_ids=true, to_apply=%region_1.0 | all-reduce | flops 4096 | bytes 32768 | tf_op jit(solution)/shard_map/pmax | solution.py:51
  63.2 2.9 %fusion.1 = f32[256,16]{0,1:T(8,128)S(1)} fusion(f32[16,256,256]{2,1,0:T(8,128)} %get-tuple-element.20, f32[256,16]{0,1:T(8,128)S(1)} %get-tuple-element.19), kind=kLoop, calls=%fused_computation.3 | loop fusion | flops 3141632 | bytes 4227072 | tf_op jit(solution)/shard_map/while/body/eval_jaxpr/reduce_sum | solution.py:39
  66.1 23.8 %all-gather.5.cloned.1.call-done = bf16[256,2048]{1,0:T(8,128)(2,1)} async-done(((bf16[16,2048]{1,0:T(8,128)(2,1)}), bf16[256,2048]{1,0:T(8,128)(2,1)}) %all-gather.5.cloned.1.call-update) | async-done | bytes 1048592 | tf_op jit(solution)/shard_map/all_gather | solution.py:23
  89.9 1.5 %copy.20 = bf16[256,2048]{0,1:T(8,128)(2,1)S(1)} copy(bf16[256,2048]{1,0:T(8,128)(2,1)} %all-gather.5.cloned.1.call-done) | data formatting | bytes 2097152 | tf_op jit(solution)/shard_map/all_gather | solution.py:23
  91.4 3.2 %fusion.7 = bf16[256,16,128]{0,2,1:T(8,128)(2,1)S(1)} fusion(bf16[256,16,128]{0,2,1:T(8,128)(2,1)S(1)} %bitcast.38, f32[16,256,256]{2,1,0:T(8,128)} %get-tuple-element.20, f32[256,16]{0,1:T(8,128)S(1)} %get-tuple-element.19, f32[256,16]{0,1:T(8,128)S(1)} %get-tuple-element.17, f32[256,16]{0,1:T(8,128)S(1)} %get-tuple-element.18), kind=kOutput, calls=%fused_computation.10 | convolution fusion | flops 273154048 | bytes 6340608 | tf_op jit(solution)/shard_map/while/body/eval_jaxpr/thk,khd->thd/dot_general | solution.py:40
  94.6 1.4 copy.22
  96.0 0.0 all-reduce.2.cloned.1.call-update
  96.0 8.2 %psum.15 = f32[256,16]{0,1:T(8,128)S(1)} all-reduce(f32[256,16]{0,1:T(8,128)S(1)} %get-tuple-element.16), channel_id=1, replica_groups=mesh['outer'=2,'inner'=16] {'outer'}, use_global_device_ids=true, to_apply=%region_4.5 | all-reduce | flops 4096 | bytes 32768 | tf_op jit(solution)/shard_map/psum | solution.py:54
  104.2 0.1 copy.23
  104.3 0.6 log_add_fusion
  104.9 30.2 %all-reduce.2.cloned.1.call-done = bf16[256,2048]{1,0:T(8,128)(2,1)} async-done(((bf16[256,2048]{1,0:T(8,128)(2,1)}), bf16[256,2048]{1,0:T(8,128)(2,1)}) %all-reduce.2.cloned.1.call-update) | async-done | bytes 1048592 | tf_op jit(solution)/shard_map/psum | solution.py:56
  135.2 0.6 div.11
  135.8 3.1 %fusion.5 = bf16[256,2048]{1,0:T(8,128)(2,1)} fusion(f32[32,8,16,128]{3,2,1,0:T(8,128)S(1)} %bitcast.37, bf16[256,2048]{1,0:T(8,128)(2,1)} %all-reduce.2.cloned.1.call-done), kind=kLoop, calls=%fused_computation.7 | loop fusion | flops 1572864 | bytes 4194304 | tf_op jit(solution)/shard_map/convert_element_type | solution.py:59
  (1 shorter events, 0.0 us)
Async XLA Ops:
  7.2 45.2 %copy-start = (bf16[256,2048]{1,0:T(8,128)(2,1)S(1)}, bf16[256,2048]{1,0:T(8,128)(2,1)}, u32[]{:S(2)}) copy-start(bf16[256,2048]{1,0:T(8,128)(2,1)} %param.3) | copy-start | bytes 3145732
  7.2 43.7 %all-gather.3.cloned.1.call-start = ((), (), s32[]{:S(2)}) async-start(), calls=%async_computation | async-start | bytes 1114112 | tf_op jit(solution)/shard_map/all_gather | solution.py:22
  7.9 82.0 %all-gather.5.cloned.1.call-start = ((), (), s32[]{:S(2)}) async-start(), calls=%async_computation.1 | async-start | bytes 1114112 | tf_op jit(solution)/shard_map/all_gather | solution.py:23
  8.7 126.5 %all-reduce.2.cloned.1.call-start = ((), (), s32[]{:S(2)}) async-start(), calls=%async_computation.2 | async-start | bytes 2097152 | tf_op jit(solution)/shard_map/psum | solution.py:56
Sparse Core Ops, SparseCore 0:
  10.2 40.6 all-gather.2
  53.0 36.8 all-gather.4
  96.2 38.9 all-reduce.1
where the time goes:
time: 146 us; the launch traced here: 145 us
  waiting for transfers between devices  97.6 us (67%)
  blocking collectives  16.3 us (11%)
  between operations  13.8 us (9%)
  other arithmetic  6.61 us (5%)
  matrix products  5.9 us (4%)
  local copies, waits for them, and re-layouts  5.08 us (3%)
    all_gather x1, waiting for transfers between devices, on_device(): key_piece = lax.all_gather(mem_keys, 'inner', axis=0, tiled=True)  42.1 us
    psum x1, waiting for transfers between devices, on_device(): lax.psum(weighted.astype(jnp.bfloat16), 'outer').astype(jnp.float32)  30.2 us
    all_gather x1, waiting for transfers between devices, on_device(): value_piece = lax.all_gather(mem_values, 'inner', axis=0, tiled=True)  23.8 us
    psum x1, blocking collectives, on_device(): total = lax.psum(group_total * factor, 'outer')  8.15 us
    pmax x1, blocking collectives, on_device(): peak = lax.pmax(group_peak, 'outer')  8.13 us
    dot_general x1, matrix products, one_block(): jnp.einsum('thk,khd->thd', raw.astype(jnp.bfloat16), value_block, preferr...  3.2 us
    convert_element_type x1, other arithmetic, on_device(): attended = (summed.reshape(row_count, HEADS, HEAD_DIM) / total[..., None]...  3.07 us
  transfers between devices with their start and end apart: 3, of which 3 were waited for; matrix products, arithmetic and copies ran while one was open for 5% of the time, Pallas kernels for 0%

commit v1 on v0

v1 whole, which is shorter than its diff:
```python
import functools
import math

import jax
import jax.numpy as jnp
from jax import lax
from jax.experimental import pallas as pl
from jax.experimental.pallas import tpu as pltpu
from jax.sharding import PartitionSpec as P

HEAD_DIM = 128
CHUNK_HEADS = 2
ENTRY_BLOCK = 512
MESH = pl.DeviceIdType.MESH


def attend(q, keys_of, values_of, entries):
    scale = 1.0 / math.sqrt(HEAD_DIM)
    to_two = scale * math.log2(math.e)
    block = math.gcd(entries, ENTRY_BLOCK)
    blocks = entries // block

    def scores_of(at):
        return lax.dot_general(
            keys_of(at, block), q, (((1,), (1,)), ((), ())), preferred_element_type=jnp.float32
        )

    def product_of(raw, at):
        return lax.dot_general(
            values_of(at, block),
            raw.astype(jnp.bfloat16),
            (((0,), (0,)), ((), ())),
            preferred_element_type=jnp.float32,
        )

    scores = scores_of(0)
    top = jnp.max(scores, axis=0, keepdims=True)
    raw = jnp.exp2((scores - top) * to_two)
    total = jnp.sum(raw, axis=0, keepdims=True)
    out = product_of(raw, 0)

    def step(number, running):
        top, total, out = running
        at = pl.multiple_of(number * block, block)
        scores = scores_of(at)
        new_top = jnp.maximum(top, jnp.max(scores, axis=0, keepdims=True))
        fading = jnp.exp2((top - new_top) * to_two)
        raw = jnp.exp2((scores - new_top) * to_two)
        total = total * fading + jnp.sum(raw, axis=0, keepdims=True)
        return new_top, total, out * fading + product_of(raw, at)

    if blocks > 1:
        top, total, out = lax.fori_loop(1, blocks, step, (top, total, out))
    return out / total, top * scale + jnp.log(total)


def kernel(
    n, Z, chunks, cw,
    q_hbm, k_ref, v_ref, out_ref, log_ref,
    qv, S, G, ob, lg,
    q_sem, x_send, x_recv, up_send, up_recv, dn_send, dn_recv,
    y_send, y_recv, c_send, c_recv, o_send, o_recv, own_sem, l_send, l_recv, l_own,
):
    o = lax.axis_index("outer")
    i = lax.axis_index("inner")
    c = lax.rem(i, 2)
    y = lax.rem(i // 2, 2)
    z = i // 4
    rows = k_ref.shape[0]
    R = rows * n
    row_of = Z * R
    lc = chunks * cw
    tokens = qv.shape[0]

    def inner_at(zz, yy, cc):
        return {"inner": (zz * 2 + yy) * 2 + cc}

    up, down = inner_at(z + 1, y, c), inner_at(z - 1, y, c)
    across, sibling = inner_at(z, 1 - y, c), inner_at(z, y, 1 - c)
    has_up, has_down = z < Z - 1, z > 0
    peers = [{"outer": lax.rem(o + d, n)} for d in range(1, n)]

    def row_start(yy, cc):
        return pl.multiple_of((cc * 2 + yy) * row_of, R)

    def block(k, zz):
        return G.at[k, pl.ds(pl.multiple_of(row_start(y, c) + zz * R, R), R), :]

    def copy(src, dst, send, recv, to):
        return pltpu.make_async_remote_copy(
            src_ref=src, dst_ref=dst, send_sem=send, recv_sem=recv, device_id=to, device_id_type=MESH
        )

    barrier = pltpu.get_barrier_semaphore()
    for to in peers + [across, sibling]:
        pl.semaphore_signal(barrier, inc=1, device_id=to, device_id_type=MESH)

    @pl.when(has_up)
    def _():
        pl.semaphore_signal(barrier, inc=1, device_id=up, device_id_type=MESH)

    @pl.when(has_down)
    def _():
        pl.semaphore_signal(barrier, inc=1, device_id=down, device_id_type=MESH)

    q_copy = pltpu.make_async_copy(
        q_hbm.at[:, pl.ds(pl.multiple_of(o * lc, 128), lc)], qv, q_sem
    )
    q_copy.start()
    for p in range(n):
        for k in range(chunks):
            at = p * lc + k * cw
            S[p, k, :, :cw] = k_ref[:, at : at + cw]
            S[p, k, :, cw:] = v_ref[:, at : at + cw]
    mine = pl.ds(pl.multiple_of(row_start(y, c) + z * R + o * rows, rows), rows)
    for k in range(chunks):
        G[k, mine, :] = S[o, k]

    pl.semaphore_wait(
        barrier, n + 1 + jnp.minimum(z, 1) + jnp.minimum(Z - 1 - z, 1)
    )

    for k in range(chunks):
        for to in peers:
            copy(S.at[to["outer"], k], G.at[k, mine, :], x_send.at[k], x_recv.at[k], to).start()

    def up_copy(k, s):
        b = block(k, z - s)
        return copy(b, b, up_send.at[k, s], up_recv.at[k, s], up)

    def down_copy(k, s):
        b = block(k, z + s)
        return copy(b, b, dn_send.at[k, s], dn_recv.at[k, s], down)

    def across_copy(k, zz):
        b = block(k, zz)
        return copy(b, b, y_send.at[k], y_recv.at[k], across)

    def line(k, yy, cc):
        return G.at[k, pl.ds(row_start(yy, cc), row_of), :]

    def sibling_copy(k, yy, which):
        b = line(k, yy, c)
        return copy(b, b, c_send.at[k, which], c_recv.at[k, which], sibling)

    def own(k):
        others = G.at[k, pl.ds(0, (n - 1) * rows), :]
        copy(others, others, x_send.at[k], x_recv.at[k], peers[0]).wait_recv()

        @pl.when(has_up)
        def _():
            up_copy(k, 0).start()

        @pl.when(has_down)
        def _():
            down_copy(k, 0).start()

        across_copy(k, z).start()

    def stage(k, s):
        @pl.when(z - s >= 0)
        def _():
            b = block(k, z - s)
            copy(b, b, up_send.at[k, s - 1], up_recv.at[k, s - 1], down).wait_recv()

            @pl.when(has_up)
            def _():
                up_copy(k, s).start()

            across_copy(k, z - s).start()

        @pl.when(z + s < Z)
        def _():
            b = block(k, z + s)
            copy(b, b, dn_send.at[k, s - 1], dn_recv.at[k, s - 1], up).wait_recv()

            @pl.when(has_down)
            def _():
                down_copy(k, s).start()

            across_copy(k, z + s).start()

        if s == Z - 1:
            sibling_copy(k, y, 0).start()

    def crossed(k):
        b = line(k, 1 - y, c)
        copy(b, b, y_send.at[k], y_recv.at[k], across).wait_recv()
        sibling_copy(k, 1 - y, 1).start()

    def out_at(k):
        return out_ref.at[:, pl.ds(pl.multiple_of(o * lc + k * cw, 128), cw)]

    def compute(k):
        if k == 0:
            q_copy.wait()
        for which, yy in ((0, y), (1, 1 - y)):
            b = line(k, yy, 1 - c)
            copy(b, b, c_send.at[k, which], c_recv.at[k, which], sibling).wait_recv()
        for h in range(cw // HEAD_DIM):
            lo = h * HEAD_DIM
            at = k * cw + lo
            out, log_total = attend(
                qv[:, at : at + HEAD_DIM],
                lambda e, size: G[k, pl.ds(e, size), lo : lo + HEAD_DIM],
                lambda e, size: G[k, pl.ds(e, size), cw + lo : cw + lo + HEAD_DIM],
                G.shape[1],
            )
            ob[k, :, lo : lo + HEAD_DIM] = out.T.astype(jnp.bfloat16)
            head = k * (cw // HEAD_DIM) + h
            lg[head : head + 1, :] = log_total
        for to in peers:
            copy(ob.at[k], out_at(k), o_send.at[k], o_recv.at[k], to).start()
        pltpu.make_async_copy(ob.at[k], out_at(k), own_sem.at[k]).start()

    events = []
    for k in range(chunks):
        events.append((3 * k, 0, k, functools.partial(own, k)))
        for s in range(1, Z):
            events.append((3 * k + 2 * s, 1, k, functools.partial(stage, k, s)))
        last = 3 * k + 2 * (Z - 1)
        events.append((last + 2, 2, k, functools.partial(crossed, k)))
        events.append((last + 3, 3, k, functools.partial(compute, k)))
    for event in sorted(events, key=lambda e: e[:3]):
        event[3]()

    log_copy = [copy(lg, log_ref.at[o], l_send, l_recv, to) for to in peers]
    for one in log_copy:
        one.start()
    log_own = pltpu.make_async_copy(lg, log_ref.at[o], l_own)
    log_own.start()

    for k in range(chunks):
        sent = G.at[k, pl.ds(0, (n - 1) * rows), :]
        copy(sent, sent, x_send.at[k], x_recv.at[k], peers[0]).wait_send()
        for s in range(Z - 1):
            @pl.when(jnp.logical_and(has_up, z - s >= 0))
            def _():
                up_copy(k, s).wait_send()

            @pl.when(jnp.logical_and(has_down, z + s < Z))
            def _():
                down_copy(k, s).wait_send()

        b = line(k, y, c)
        copy(b, b, y_send.at[k], y_recv.at[k], across).wait_send()
        sibling_copy(k, y, 0).wait_send()
        sibling_copy(k, 1 - y, 1).wait_send()
        pltpu.make_async_copy(ob.at[k], out_at(k), own_sem.at[k]).wait()
        some = out_ref.at[:, pl.ds(0, (n - 1) * cw)]
        whole = copy(some, some, o_send.at[k], o_recv.at[k], peers[0])
        whole.wait_send()
        whole.wait_recv()
    log_own.wait()
    some = log_ref.at[pl.ds(0, n - 1)]
    whole = copy(some, some, l_send, l_recv, peers[0])
    whole.wait_send()
    whole.wait_recv()


def on_device(n, inner, queries, mem_keys, mem_values):
    tokens, columns = queries.shape
    rows = mem_keys.shape[0]
    Z = inner // 4
    heads = columns // HEAD_DIM
    lh = heads // n
    lc = lh * HEAD_DIM
    cw = math.gcd(lh, CHUNK_HEADS) * HEAD_DIM
    chunks = lc // cw
    R = rows * n
    entries = inner * R
    dma = pltpu.SemaphoreType.DMA
    attended, logs = pl.pallas_call(
        functools.partial(kernel, n, Z, chunks, cw),
        out_shape=(
            jax.ShapeDtypeStruct((tokens, columns), jnp.bfloat16),
            jax.ShapeDtypeStruct((n, lh, tokens), jnp.float32),
        ),
        in_specs=[
            pl.BlockSpec(memory_space=pl.ANY),
            pl.BlockSpec(memory_space=pltpu.VMEM),
            pl.BlockSpec(memory_space=pltpu.VMEM),
        ],
        out_specs=(pl.BlockSpec(memory_space=pl.ANY), pl.BlockSpec(memory_space=pl.ANY)),
        scratch_shapes=[
            pltpu.VMEM((tokens, lc), jnp.bfloat16),
            pltpu.VMEM((n, chunks, rows, 2 * cw), jnp.bfloat16),
            pltpu.VMEM((chunks, entries, 2 * cw), jnp.bfloat16),
            pltpu.VMEM((chunks, tokens, cw), jnp.bfloat16),
            pltpu.VMEM((lh, tokens), jnp.float32),
            dma,
            dma((chunks,)), dma((chunks,)),
            dma((chunks, Z)), dma((chunks, Z)), dma((chunks, Z)), dma((chunks, Z)),
            dma((chunks,)), dma((chunks,)),
            dma((chunks, 2)), dma((chunks, 2)),
            dma((chunks,)), dma((chunks,)), dma((chunks,)),
            dma, dma, dma,
        ],
        compiler_params=pltpu.CompilerParams(
            collective_id=0, has_side_effects=True, vmem_limit_bytes=40 * 2**20
        ),
        cost_estimate=pl.CostEstimate(
            flops=4 * tokens * entries * lc,
            bytes_accessed=4 * tokens * columns,
            transcendentals=tokens * entries * lh,
        ),
    )(queries, mem_keys, mem_values)
    return attended, logs.reshape(heads, tokens).T


def solution(mesh):
    in_specs = (P("inner", None), P(("outer", "inner"), None), P(("outer", "inner"), None))
    out_specs = (P("inner", None), P("inner", None))
    return jax.shard_map(
        functools.partial(on_device, mesh.shape["outer"], mesh.shape["inner"]),
        mesh=mesh, in_specs=in_specs, out_specs=out_specs, check_vma=False,
    )
```

time: 146 us -> 43 us (0.29)
  waiting for transfers between devices: 97.6 us -> 0 us
  Pallas kernels: 0 us -> 37.6 us
  blocking collectives: 16.3 us -> 0 us
  between operations: 13.8 us -> 0.65 us
  other arithmetic: 6.61 us -> 0 us
  matrix products: 5.9 us -> 0 us
    all_gather x2 -> x0, waiting for transfers between devices: 65.9 us -> none  [the longest x1 42.1 us: on_device(): key_piece = lax.all_gather(mem_keys, 'inner', axis=0, tiled=True)]
    pallas_call x0 -> x1, Pallas kernels: none -> 37.6 us  [on_device(): pl.pallas_call(functools.partial(kernel, n, Z, chunks, cw), out_shape=(ja...]
    psum x1 -> x0, waiting for transfers between devices: 30.2 us -> none  [on_device(): lax.psum(weighted.astype(jnp.bfloat16), 'outer').astype(jnp.float32)]
    psum x1 -> x0, blocking collectives: 8.15 us -> none  [on_device(): total = lax.psum(group_total * factor, 'outer')]
    pmax x1 -> x0, blocking collectives: 8.13 us -> none  [on_device(): peak = lax.pmax(group_peak, 'outer')]
    dot_general x2 -> x0, matrix products: 5.9 us -> none  [the longest x1 3.2 us: one_block(): jnp.einsum('thk,khd->thd', raw.astype(jnp.bfloat16), value_block, preferr...]
    unnamed x2 -> x8, local copies, waits for them, and re-layouts: 0.01 us -> 4.47 us
    convert_element_type x1 -> x0, other arithmetic: 3.07 us -> none  [on_device(): attended = (summed.reshape(row_count, HEADS, HEAD_DIM) / total[..., None]...]
  transfers between devices with their start and end apart: 3 -> 0, of which waited for: 3 -> 0; matrix products, arithmetic and copies ran while one was open for 5% -> 0% of each run, Pallas kernels for 0% -> 0%
where the time goes in v1:
time: 43 us; the launch traced here: 42.8 us
  Pallas kernels  37.6 us (87%)
  local copies, waits for them, and re-layouts  4.47 us (10%)
  between operations  0.65 us (2%)
    pallas_call x1, Pallas kernels, on_device(): pl.pallas_call(functools.partial(kernel, n, Z, chunks, cw), out_shape=(ja...  37.6 us
    unnamed x8, local copies, waits for them, and re-layouts  4.47 us

profile of v1, /device:TPU:0, one launch (start us, length us, event | category | flops | bytes accessed | tf_op | source)
XLA Modules:
  0.0 42.8 jit_solution(14620804712172481107)
XLA Ops:
  0.6 0.0 copy-start
  0.6 1.2 %copy-done = bf16[256,2048]{1,0:T(8,128)(2,1)S(1)} copy-done((bf16[256,2048]{1,0:T(8,128)(2,1)S(1)}, bf16[256,2048]{1,0:T(8,128)(2,1)}, u32[]{:S(2)}) %copy-start) | copy-done | bytes 1048600
  1.9 0.0 copy-start.1
  1.9 0.8 %copy-done.1 = bf16[16,2048]{1,0:T(8,128)(2,1)S(1)} copy-done((bf16[16,2048]{1,0:T(8,128)(2,1)S(1)}, bf16[16,2048]{1,0:T(8,128)(2,1)}, u32[]{:S(2)}) %copy-start.1) | copy-done | bytes 65560
  2.7 0.0 copy-start.2
  2.7 0.8 %copy-done.2 = bf16[16,2048]{1,0:T(8,128)(2,1)S(1)} copy-done((bf16[16,2048]{1,0:T(8,128)(2,1)S(1)}, bf16[16,2048]{1,0:T(8,128)(2,1)}, u32[]{:S(2)}) %copy-start.2) | copy-done | bytes 65560
  3.5 37.6 %shard_map.50 = (bf16[256,2048]{1,0:T(8,128)(2,1)S(1)}, f32[2,8,256]{2,1,0:T(8,128)S(1)}) custom-call(bf16[256,2048]{1,0:T(8,128)(2,1)S(1)} %copy-done, bf16[16,2048]{1,0:T(8,128)(2,1)S(1)} %copy-done.1, bf16[16,2048]{1,0:T(8,128)(2,1)S(1)} %copy-done.2), custom_call_target="tpu_custom_call" | custom-call | flops 536870912 | bytes 2097152 | tf_op jit(solution)/shard_map/pallas_call | solution.py:273
  41.2 1.0 %copy.7 = bf16[256,2048]{1,0:T(8,128)(2,1)} copy(bf16[256,2048]{1,0:T(8,128)(2,1)S(1)} %get-tuple-element.8) | data formatting | bytes 2097152
  42.2 0.6 %copy.8 = f32[256,16]{0,1:T(8,128)} copy(f32[256,16]{0,1:T(8,128)S(1)} %bitcast.3) | data formatting | bytes 32768
Async XLA Ops:
  0.6 1.2 %copy-start = (bf16[256,2048]{1,0:T(8,128)(2,1)S(1)}, bf16[256,2048]{1,0:T(8,128)(2,1)}, u32[]{:S(2)}) copy-start(bf16[256,2048]{1,0:T(8,128)(2,1)} %q_hbm.1) | copy-start | bytes 3145732
  1.9 0.8 %copy-start.1 = (bf16[16,2048]{1,0:T(8,128)(2,1)S(1)}, bf16[16,2048]{1,0:T(8,128)(2,1)}, u32[]{:S(2)}) copy-start(bf16[16,2048]{1,0:T(8,128)(2,1)} %k_ref.1) | copy-start | bytes 196612
  2.7 0.8 %copy-start.2 = (bf16[16,2048]{1,0:T(8,128)(2,1)S(1)}, bf16[16,2048]{1,0:T(8,128)(2,1)}, u32[]{:S(2)}) copy-start(bf16[16,2048]{1,0:T(8,128)(2,1)} %v_ref.1) | copy-start | bytes 196612

commit v2 on v1

--- a/solution.py
+++ b/solution.py
@@ -10,6 +10,7 @@
 
 HEAD_DIM = 128
 CHUNK_HEADS = 2
+CHUNK_STEP, STAGE_STEP = 1, 4
 ENTRY_BLOCK = 512
 MESH = pl.DeviceIdType.MESH
 
@@ -56,8 +57,8 @@
 
 def kernel(
     n, Z, chunks, cw,
-    q_hbm, k_ref, v_ref, out_ref, log_ref,
-    qv, S, G, ob, lg,
+    q_hbm, k_hbm, v_hbm, out_ref, log_ref,
+    k_ref, v_ref, k_sem, v_sem, qv, S, G, ob, lg,
     q_sem, x_send, x_recv, up_send, up_recv, dn_send, dn_recv,
     y_send, y_recv, c_send, c_recv, o_send, o_recv, own_sem, l_send, l_recv, l_own,
 ):
@@ -91,6 +92,10 @@
             src_ref=src, dst_ref=dst, send_sem=send, recv_sem=recv, device_id=to, device_id_type=MESH
         )
 
+    k_copy = pltpu.make_async_copy(k_hbm, k_ref, k_sem)
+    v_copy = pltpu.make_async_copy(v_hbm, v_ref, v_sem)
+    k_copy.start()
+    v_copy.start()
     barrier = pltpu.get_barrier_semaphore()
     for to in peers + [across, sibling]:
         pl.semaphore_signal(barrier, inc=1, device_id=to, device_id_type=MESH)
@@ -107,6 +112,8 @@
         q_hbm.at[:, pl.ds(pl.multiple_of(o * lc, 128), lc)], qv, q_sem
     )
     q_copy.start()
+    k_copy.wait()
+    v_copy.wait()
     for p in range(n):
         for k in range(chunks):
             at = p * lc + k * cw
@@ -215,10 +222,10 @@
 
     events = []
     for k in range(chunks):
-        events.append((3 * k, 0, k, functools.partial(own, k)))
+        events.append((CHUNK_STEP * k, 0, k, functools.partial(own, k)))
         for s in range(1, Z):
-            events.append((3 * k + 2 * s, 1, k, functools.partial(stage, k, s)))
-        last = 3 * k + 2 * (Z - 1)
+            events.append((CHUNK_STEP * k + STAGE_STEP * s, 1, k, functools.partial(stage, k, s)))
+        last = CHUNK_STEP * k + STAGE_STEP * (Z - 1)
         events.append((last + 2, 2, k, functools.partial(crossed, k)))
         events.append((last + 3, 3, k, functools.partial(compute, k)))
     for event in sorted(events, key=lambda e: e[:3]):
@@ -277,12 +284,16 @@
             jax.ShapeDtypeStruct((n, lh, tokens), jnp.float32),
         ),
         in_specs=[
-            pl.BlockSpec(memory_space=pl.ANY),
-            pl.BlockSpec(memory_space=pltpu.VMEM),
-            pl.BlockSpec(memory_space=pltpu.VMEM),
+            pl.BlockSpec(memory_space=pltpu.HBM),
+            pl.BlockSpec(memory_space=pltpu.HBM),
+            pl.BlockSpec(memory_space=pltpu.HBM),
         ],
         out_specs=(pl.BlockSpec(memory_space=pl.ANY), pl.BlockSpec(memory_space=pl.ANY)),
         scratch_shapes=[
+            pltpu.VMEM(mem_keys.shape, jnp.bfloat16),
+            pltpu.VMEM(mem_keys.shape, jnp.bfloat16),
+            dma,
+            dma,
             pltpu.VMEM((tokens, lc), jnp.bfloat16),
             pltpu.VMEM((n, chunks, rows, 2 * cw), jnp.bfloat16),
             pltpu.VMEM((chunks, entries, 2 * cw), jnp.bfloat16),

time: 43 us -> 41.1 us (0.956)
  Pallas kernels: 37.6 us -> 35.7 us
    pallas_call x1, Pallas kernels: 37.6 us -> 35.7 us  [on_device(): pl.pallas_call(functools.partial(kernel, n, Z, chunks, cw), out_shape=(ja...]
where the time goes in v2:
time: 41.1 us; the launch traced here: 40.8 us
  Pallas kernels  35.7 us (87%)
  local copies, waits for them, and re-layouts  4.47 us (11%)
  between operations  0.65 us (2%)
    pallas_call x1, Pallas kernels, on_device(): pl.pallas_call(functools.partial(kernel, n, Z, chunks, cw), out_shape=(ja...  35.7 us
    unnamed x8, local copies, waits for them, and re-layouts  4.47 us

profile of v2, /device:TPU:0, one launch (start us, length us, event | category | flops | bytes accessed | tf_op | source)
XLA Modules:
  0.0 40.8 jit_solution(4887527124363453339)
XLA Ops:
  0.6 0.0 copy-start
  0.6 1.2 %copy-done = bf16[256,2048]{1,0:T(8,128)(2,1)S(1)} copy-done((bf16[256,2048]{1,0:T(8,128)(2,1)S(1)}, bf16[256,2048]{1,0:T(8,128)(2,1)}, u32[]{:S(2)}) %copy-start) | copy-done | bytes 1048600
  1.9 0.0 copy-start.1
  1.9 0.8 %copy-done.1 = bf16[16,2048]{1,0:T(8,128)(2,1)S(1)} copy-done((bf16[16,2048]{1,0:T(8,128)(2,1)S(1)}, bf16[16,2048]{1,0:T(8,128)(2,1)}, u32[]{:S(2)}) %copy-start.1) | copy-done | bytes 65560
  2.7 0.0 copy-start.2
  2.7 0.8 %copy-done.2 = bf16[16,2048]{1,0:T(8,128)(2,1)S(1)} copy-done((bf16[16,2048]{1,0:T(8,128)(2,1)S(1)}, bf16[16,2048]{1,0:T(8,128)(2,1)}, u32[]{:S(2)}) %copy-start.2) | copy-done | bytes 65560
  3.5 35.7 %shard_map.50 = (bf16[256,2048]{1,0:T(8,128)(2,1)S(1)}, f32[2,8,256]{2,1,0:T(8,128)S(1)}) custom-call(bf16[256,2048]{1,0:T(8,128)(2,1)S(1)} %copy-done, bf16[16,2048]{1,0:T(8,128)(2,1)S(1)} %copy-done.1, bf16[16,2048]{1,0:T(8,128)(2,1)S(1)} %copy-done.2), custom_call_target="tpu_custom_call" | custom-call | flops 536870912 | bytes 2097152 | tf_op jit(solution)/shard_map/pallas_call | solution.py:280
  39.2 1.0 %copy.7 = bf16[256,2048]{1,0:T(8,128)(2,1)} copy(bf16[256,2048]{1,0:T(8,128)(2,1)S(1)} %get-tuple-element.8) | data formatting | bytes 2097152
  40.2 0.6 %copy.8 = f32[256,16]{0,1:T(8,128)} copy(f32[256,16]{0,1:T(8,128)S(1)} %bitcast.3) | data formatting | bytes 32768
Async XLA Ops:
  0.6 1.2 %copy-start = (bf16[256,2048]{1,0:T(8,128)(2,1)S(1)}, bf16[256,2048]{1,0:T(8,128)(2,1)}, u32[]{:S(2)}) copy-start(bf16[256,2048]{1,0:T(8,128)(2,1)} %q_hbm.1) | copy-start | bytes 3145732
  1.9 0.8 %copy-start.1 = (bf16[16,2048]{1,0:T(8,128)(2,1)S(1)}, bf16[16,2048]{1,0:T(8,128)(2,1)}, u32[]{:S(2)}) copy-start(bf16[16,2048]{1,0:T(8,128)(2,1)} %k_hbm.1) | copy-start | bytes 196612
  2.7 0.8 %copy-start.2 = (bf16[16,2048]{1,0:T(8,128)(2,1)S(1)}, bf16[16,2048]{1,0:T(8,128)(2,1)}, u32[]{:S(2)}) copy-start(bf16[16,2048]{1,0:T(8,128)(2,1)} %v_hbm.1) | copy-start | bytes 196612

commit v3 on v2

--- a/solution.py
+++ b/solution.py
@@ -150,19 +150,32 @@
         b = line(k, yy, c)
         return copy(b, b, c_send.at[k, which], c_recv.at[k, which], sibling)
 
+    def piece(k, d):
+        at = row_start(y, c) + z * R + lax.rem(o + d, n) * rows
+        return G.at[k, pl.ds(pl.multiple_of(at, rows), rows), :]
+
+    def send_piece(k, d):
+        b = piece(k, d)
+
+        @pl.when(has_up)
+        def _():
+            copy(b, b, up_send.at[k, 0], up_recv.at[k, 0], up).start()
+
+        @pl.when(has_down)
+        def _():
+            copy(b, b, dn_send.at[k, 0], dn_recv.at[k, 0], down).start()
+
+        copy(b, b, y_send.at[k], y_recv.at[k], across).start()
+
+    for k in range(chunks):
+        send_piece(k, 0)
+
     def own(k):
         others = G.at[k, pl.ds(0, (n - 1) * rows), :]
         copy(others, others, x_send.at[k], x_recv.at[k], peers[0]).wait_recv()
 
-        @pl.when(has_up)
-        def _():
-            up_copy(k, 0).start()
-
-        @pl.when(has_down)
-        def _():
-            down_copy(k, 0).start()
-
-        across_copy(k, z).start()
+        for d in range(1, n):
+            send_piece(k, d)
 
     def stage(k, s):
         @pl.when(z - s >= 0)
@@ -215,9 +228,11 @@
             )
             ob[k, :, lo : lo + HEAD_DIM] = out.T.astype(jnp.bfloat16)
             head = k * (cw // HEAD_DIM) + h
+            column = pl.multiple_of(o * lc + at, HEAD_DIM)
+            place = out_ref.at[:, pl.ds(column, HEAD_DIM)]
+            for to in peers:
+                copy(ob.at[k, :, lo : lo + HEAD_DIM], place, o_send.at[k], o_recv.at[k], to).start()
             lg[head : head + 1, :] = log_total
-        for to in peers:
-            copy(ob.at[k], out_at(k), o_send.at[k], o_recv.at[k], to).start()
         pltpu.make_async_copy(ob.at[k], out_at(k), own_sem.at[k]).start()
 
     events = []

time: 41.1 us -> 40.5 us (0.985)
  Pallas kernels: 35.7 us -> 35.1 us
    pallas_call x1, Pallas kernels: 35.7 us -> 35.1 us  [on_device(): pl.pallas_call(functools.partial(kernel, n, Z, chunks, cw), out_shape=(ja...]
where the time goes in v3:
time: 40.5 us; the launch traced here: 40.2 us
  Pallas kernels  35.1 us (87%)
  local copies, waits for them, and re-layouts  4.47 us (11%)
  between operations  0.65 us (2%)
    pallas_call x1, Pallas kernels, on_device(): pl.pallas_call(functools.partial(kernel, n, Z, chunks, cw), out_shape=(ja...  35.1 us
    unnamed x8, local copies, waits for them, and re-layouts  4.47 us

profile of v3, /device:TPU:0, one launch (start us, length us, event | category | flops | bytes accessed | tf_op | source)
XLA Modules:
  0.0 40.2 jit_solution(6772790896784132357)
XLA Ops:
  0.6 0.0 copy-start
  0.6 1.2 %copy-done = bf16[256,2048]{1,0:T(8,128)(2,1)S(1)} copy-done((bf16[256,2048]{1,0:T(8,128)(2,1)S(1)}, bf16[256,2048]{1,0:T(8,128)(2,1)}, u32[]{:S(2)}) %copy-start) | copy-done | bytes 1048600
  1.9 0.0 copy-start.1
  1.9 0.8 %copy-done.1 = bf16[16,2048]{1,0:T(8,128)(2,1)S(1)} copy-done((bf16[16,2048]{1,0:T(8,128)(2,1)S(1)}, bf16[16,2048]{1,0:T(8,128)(2,1)}, u32[]{:S(2)}) %copy-start.1) | copy-done | bytes 65560
  2.7 0.0 copy-start.2
  2.7 0.8 %copy-done.2 = bf16[16,2048]{1,0:T(8,128)(2,1)S(1)} copy-done((bf16[16,2048]{1,0:T(8,128)(2,1)S(1)}, bf16[16,2048]{1,0:T(8,128)(2,1)}, u32[]{:S(2)}) %copy-start.2) | copy-done | bytes 65560
  3.5 35.1 %shard_map.50 = (bf16[256,2048]{1,0:T(8,128)(2,1)S(1)}, f32[2,8,256]{2,1,0:T(8,128)S(1)}) custom-call(bf16[256,2048]{1,0:T(8,128)(2,1)S(1)} %copy-done, bf16[16,2048]{1,0:T(8,128)(2,1)S(1)} %copy-done.1, bf16[16,2048]{1,0:T(8,128)(2,1)S(1)} %copy-done.2), custom_call_target="tpu_custom_call" | custom-call | flops 536870912 | bytes 2097152 | tf_op jit(solution)/shard_map/pallas_call | solution.py:295
  38.6 1.0 %copy.7 = bf16[256,2048]{1,0:T(8,128)(2,1)} copy(bf16[256,2048]{1,0:T(8,128)(2,1)S(1)} %get-tuple-element.8) | data formatting | bytes 2097152
  39.6 0.6 %copy.8 = f32[256,16]{0,1:T(8,128)} copy(f32[256,16]{0,1:T(8,128)S(1)} %bitcast.3) | data formatting | bytes 32768
Async XLA Ops:
  0.6 1.2 %copy-start = (bf16[256,2048]{1,0:T(8,128)(2,1)S(1)}, bf16[256,2048]{1,0:T(8,128)(2,1)}, u32[]{:S(2)}) copy-start(bf16[256,2048]{1,0:T(8,128)(2,1)} %q_hbm.1) | copy-start | bytes 3145732
  1.9 0.8 %copy-start.1 = (bf16[16,2048]{1,0:T(8,128)(2,1)S(1)}, bf16[16,2048]{1,0:T(8,128)(2,1)}, u32[]{:S(2)}) copy-start(bf16[16,2048]{1,0:T(8,128)(2,1)} %k_hbm.1) | copy-start | bytes 196612
  2.7 0.8 %copy-start.2 = (bf16[16,2048]{1,0:T(8,128)(2,1)S(1)}, bf16[16,2048]{1,0:T(8,128)(2,1)}, u32[]{:S(2)}) copy-start(bf16[16,2048]{1,0:T(8,128)(2,1)} %v_hbm.1) | copy-start | bytes 196612
